TPU v7x, 256 devices: a whole 4x4x8 slice. The times are simulated.
256 devices in a mesh: inp: 8 (over z), wt: 8 (over x_lo, y), out: 4 (over x_hi, core).
Axes of the slice: x: 4 (x_hi: 2, x_lo: 2; x = x_hi * 2 + x_lo), y: 4, z: 8, core: 2. Of those that a mesh axis runs over, the one named last changes fastest.
Arguments:
- tokens: bfloat16 [1536, 8192], P(('inp', 'out'), 'wt'), may hold values from -6 to 6
- gate_weight: bfloat16 [8192, 28672], P('wt', ('inp', 'out')), may hold values from -0.0625 to 0.0625
- up_weight: bfloat16 [8192, 28672], P('wt', ('inp', 'out')), may hold values from -0.0625 to 0.0625
- down_weight: bfloat16 [28672, 8192], P(('inp', 'out'), 'wt'), may hold values from -0.03125 to 0.03125
Outputs:
- mixed: bfloat16 [1536, 8192], P(('inp', 'out'), 'wt')
All inputs are finite; a program needn't handle non-finite values.
Results may differ from a plain program's by a relative error of at most 0.0049.
Values may be sent and summed in bfloat16 or wider, within the bound.
A program may use at most 128 MiB of HBM per device.

v0:
```python
import jax
import jax.numpy as jnp
from jax import lax
from jax.sharding import PartitionSpec as P


def shards(tokens, gate_weight, up_weight, down_weight):
    all_tokens = lax.all_gather(tokens, ("inp", "out"), axis=0, tiled=True)
    gate_part = jnp.dot(all_tokens, gate_weight, preferred_element_type=jnp.float32)
    up_part = jnp.dot(all_tokens, up_weight, preferred_element_type=jnp.float32)
    gate_own, up_own = (
        lax.psum_scatter(gate_part, "wt", scatter_dimension=0, tiled=True),
        lax.psum_scatter(up_part, "wt", scatter_dimension=0, tiled=True),
    )
    hidden_own = (gate_own * jax.nn.sigmoid(gate_own) * up_own).astype(jnp.bfloat16)
    hidden_full = lax.all_gather(hidden_own, "wt", axis=0, tiled=True)
    return lax.psum_scatter(
        jnp.dot(hidden_full, down_weight, preferred_element_type=jnp.float32),
        ("inp", "out"),
        scatter_dimension=0,
        tiled=True,
    ).astype(jnp.bfloat16)


def solution(mesh):
    return jax.shard_map(
        shards,
        mesh=mesh,
        in_specs=(
            P(("inp", "out"), "wt"),
            P("wt", ("inp", "out")),
            P("wt", ("inp", "out")),
            P(("inp", "out"), "wt"),
        ),
        out_specs=P(("inp", "out"), "wt"),
        check_vma=False,
    )
```

profile of v0, /device:TPU:1, one launch (start us, length us, event | category | flops | bytes accessed | tf_op | source)
XLA Modules:
  0.0 434.4 jit_solution(3911826480655849599)
XLA Ops:
  6.5 0.0 copy-start
  6.5 0.0 all-gather.3.cloned.1.call-start
  6.5 0.7 all-gather.3.cloned.1.call-update
  7.3 0.0 reduce-scatter.6.cloned.1.call-start
  7.3 90.3 %all-gather.3.cloned.1.call-done = bf16[1536,1024]{1,0:T(8,128)(2,1)} async-done(((bf16[48,1024]{1,0:T(8,128)(2,1)}), bf16[1536,1024]{1,0:T(8,128)(2,1)}) %all-gather.3.cloned.1.call-update) | async-done | bytes 3145744 | tf_op jit(solution)/shard_map/all_gather | solution.py:8
  97.6 8.3 %fusion.1 = f32[1536,896]{1,0:T(8,128)} fusion(bf16[1536,1024]{1,0:T(8,128)(2,1)} %all-gather.3.cloned.1.call-done, bf16[1024,896]{1,0:T(8,128)(2,1)} %param.6), kind=kOutput, calls=%fused_computation.2 | convolution fusion | flops 2818572288 | bytes 10485760 | tf_op jit(solution)/shard_map/dot_general | solution.py:10
  105.9 0.0 reduce-scatter.6.cloned.1.call-update
  106.0 0.0 reduce-scatter.4.cloned.1.call-start
  106.0 8.4 %fusion = f32[1536,896]{1,0:T(8,128)} fusion(bf16[1536,1024]{1,0:T(8,128)(2,1)} %all-gather.3.cloned.1.call-done, bf16[1024,896]{1,0:T(8,128)(2,1)} %param.5), kind=kOutput, calls=%fused_computation.1 | convolution fusion | flops 2818572288 | bytes 10485760 | tf_op jit(solution)/shard_map/dot_general | solution.py:9
  114.4 0.0 reduce-scatter.4.cloned.1.call-update
  114.4 0.0 all-gather.5.cloned.1.call-start
  114.4 56.2 %reduce-scatter.6.cloned.1.call-done = f32[192,896]{1,0:T(8,128)} async-done(((f32[1536,896]{1,0:T(8,128)}), f32[192,896]{1,0:T(8,128)}) %reduce-scatter.6.cloned.1.call-update) | async-done | bytes 688144 | tf_op jit(solution)/shard_map/reduce_scatter | solution.py:13
  170.6 69.4 %reduce-scatter.4.cloned.1.call-done = f32[192,896]{1,0:T(8,128)} async-done(((f32[1536,896]{1,0:T(8,128)}), f32[192,896]{1,0:T(8,128)}) %reduce-scatter.4.cloned.1.call-update) | async-done | bytes 688144 | tf_op jit(solution)/shard_map/reduce_scatter | solution.py:12
  240.0 2.2 multiply_convert_fusion
  242.3 0.0 all-gather.5.cloned.1.call-update
  242.3 0.0 reduce-scatter.8.cloned.1.call-start
  242.3 41.3 %all-gather.5.cloned.1.call-done = bf16[1536,896]{1,0:T(8,128)(2,1)} async-done(((bf16[192,896]{1,0:T(8,128)(2,1)}), bf16[1536,896]{1,0:T(8,128)(2,1)}) %all-gather.5.cloned.1.call-update) | async-done | bytes 2752528 | tf_op jit(solution)/shard_map/all_gather | solution.py:16
  283.6 0.0 copy-done
  283.6 7.1 %fusion.2 = f32[1536,1024]{1,0:T(8,128)} fusion(bf16[1536,896]{1,0:T(8,128)(2,1)} %all-gather.5.cloned.1.call-done, bf16[896,1024]{1,0:T(8,128)(2,1)S(1)} %copy-done), kind=kOutput, calls=%fused_computation.3 | convolution fusion | flops 2818572288 | bytes 10878976 | tf_op jit(solution)/shard_map/dot_general | solution.py:18
  290.8 0.0 reduce-scatter.8.cloned.1.call-update
  290.8 135.5 %reduce-scatter.8.cloned.1.call-done = f32[48,1024]{1,0:T(8,128)} async-done(((f32[1536,1024]{1,0:T(8,128)}), f32[48,1024]{1,0:T(8,128)}) %reduce-scatter.8.cloned.1.call-update) | async-done | bytes 196624 | tf_op jit(solution)/shard_map/reduce_scatter | solution.py:17
  426.3 1.6 convert_element_type.7
Async XLA Ops:
  6.5 277.1 %copy-start = (bf16[896,1024]{1,0:T(8,128)(2,1)S(1)}, bf16[896,1024]{1,0:T(8,128)(2,1)}, u32[]{:S(2)}) copy-start(bf16[896,1024]{1,0:T(8,128)(2,1)} %param.7) | copy-start | bytes 5505028
  6.5 91.1 %all-gather.3.cloned.1.call-start = ((), (), s32[]{:S(2)}) async-start(), calls=%async_computation.3 | async-start | bytes 3244032 | tf_op jit(solution)/shard_map/all_gather | solution.py:8
  7.3 163.3 %reduce-scatter.6.cloned.1.call-start = ((), (), s32[]{:S(2)}) async-start(), calls=%async_computation.5 | async-start | bytes 6193152 | tf_op jit(solution)/shard_map/reduce_scatter | solution.py:13
  106.0 134.1 %reduce-scatter.4.cloned.1.call-start = ((), (), s32[]{:S(2)}) async-start(), calls=%async_computation.4 | async-start | bytes 6193152 | tf_op jit(solution)/shard_map/reduce_scatter | solution.py:12
  114.4 169.2 %all-gather.5.cloned.1.call-start = ((), (), s32[]{:S(2)}) async-start(), calls=%async_computation.6 | async-start | bytes 3096576 | tf_op jit(solution)/shard_map/all_gather | solution.py:16
  242.3 184.0 %reduce-scatter.8.cloned.1.call-start = ((), (), s32[]{:S(2)}) async-start(), calls=%async_computation.7 | async-start | bytes 6488064 | tf_op jit(solution)/shard_map/reduce_scatter | solution.py:17
Sparse Core Ops, SparseCore 0:
  10.1 87.4 all-gather.2
  106.1 64.4 reduce-scatter.5
  173.2 66.8 reduce-scatter.3
  242.4 41.1 all-gather.4
  290.9 135.3 reduce-scatter.7
where the time goes:
time: 438 us; the launch traced here: 434 us
  waiting for transfers between devices  394 us (90%)
  matrix products  23.8 us (5%)
  between operations  13.1 us (3%)
    reduce_scatter x1, waiting for transfers between devices, shards(): lax.psum_scatter(jnp.dot(hidden_full, down_weight, preferred_element_type...  136 us
    all_gather x1, waiting for transfers between devices, shards(): all_tokens = lax.all_gather(tokens, ('inp', 'out'), axis=0, tiled=True)  90.3 us
    reduce_scatter x1, waiting for transfers between devices, shards(): lax.psum_scatter(gate_part, 'wt', scatter_dimension=0, tiled=True)  69.4 us
    reduce_scatter x1, waiting for transfers between devices, shards(): lax.psum_scatter(up_part, 'wt', scatter_dimension=0, tiled=True)  56.2 us
    all_gather x1, waiting for transfers between devices, shards(): hidden_full = lax.all_gather(hidden_own, 'wt', axis=0, tiled=True)  41.3 us
  transfers between devices with their start and end apart: 5, of which 5 were waited for; matrix products, arithmetic and copies ran while one was open for 2% of the time, Pallas kernels for 0%

commit v1 on v0

v1 whole, which is shorter than its diff:
```python
import jax
import jax.numpy as jnp
from jax import lax
from jax.experimental import pallas as pl
from jax.experimental.pallas import tpu as pltpu
from jax.sharding import PartitionSpec as P

MESH = pl.DeviceIdType.MESH
BF, F32 = jnp.bfloat16, jnp.float32

ROWS = 48
KB = 1024
FB = 896
HALF = 512
CHUNKS = 4
OFFS = ((0, 1), (-2, 3), (4, -3), (-1, 2))
STAGE_AT = dict(xf=-1.0, m1=0.0, s2=9.0, s3=14.0, s4=18.0, a2=21.0, a3=24.0, m2=27.0, g1=30.0)
CHUNK_AT = (0.0, 5.0, 18.0, 31.0)
N_SEM = 192


def kernel(tok, wg, wu, wd, out, w1, w2, x, p16, p32, gr1, sb, gr2, gs, gx, ux, q16, q32, ur1, uv, ur2, h, o32, cr, zs, zr, own,
           ssem, rsem, lsem):
    z = lax.axis_index("inp")
    wt = lax.axis_index("wt")
    ot = lax.axis_index("out")
    a, y = wt // 4, wt % 4
    xh, core = ot // 2, ot % 2
    na = 1 - a
    yr, yl, yo = (y + 1) % 4, (y + 3) % 4, (y + 2) % 4

    def dev(dz=0, dx=0, dc=0):
        return (lax.rem(z + dz + 8, 8), wt, (xh + dx) % 2 * 2 + (core + dc) % 2)

    sibling = dev(dc=1)
    right, left, across = (z, a * 4 + yr, ot), (z, a * 4 + yl, ot), (z, na * 4 + y, ot)

    loads = [
        pltpu.make_async_copy(tok, x.at[0, 0, 0, 0], lsem.at[0]),
        pltpu.make_async_copy(wg, w1.at[:, pl.ds(0, FB)], lsem.at[1]),
        pltpu.make_async_copy(wu, w1.at[:, pl.ds(FB, FB)], lsem.at[2]),
        pltpu.make_async_copy(wd, w2, lsem.at[3]),
    ]
    for load in loads:
        load.start()

    barrier = pltpu.get_barrier_semaphore()
    peers = [sibling, right, left, across]
    for dz in range(8):
        for dx in range(2):
            if dz or dx:
                peers.append(dev(dz=dz, dx=dx))
    for peer in peers:
        pl.semaphore_signal(barrier, inc=1, device_id=peer, device_id_type=MESH)
    pl.semaphore_wait(barrier, len(peers))

    copies = {}

    def send(name, src, dst, to):
        i = len(copies)
        cp = pltpu.make_async_remote_copy(
            src_ref=src, dst_ref=dst, send_sem=ssem.at[i], recv_sem=rsem.at[i], device_id=to, device_id_type=MESH
        )
        cp.start()
        copies[name] = cp

    def got(*names):
        for name in names:
            copies[name].wait_recv()

    loads[0].wait()
    send("x_hi", x.at[0, 0, 0, 0], x.at[0, 0, 1, 0], dev(dx=1))
    send("x_c0", x.at[0, 0, 0, 0], x.at[0, 0, 0, 1], sibling)
    got("x_hi")
    for c in range(CHUNKS):
        for zi in range(2):
            o = OFFS[c][zi]
            if o:
                send(("x", c, zi), x.at[0, 0, :, 0], x.at[c, zi, :, 0], dev(dz=-o))
    send("x_c1", x.at[0, 0, 1, 0], x.at[0, 0, 1, 1], sibling)

    def xf(c):
        for zi in range(2):
            if OFFS[c][zi]:
                got(("x", c, zi))
                send(("xc", c, zi), x.at[c, zi, :, 0], x.at[c, zi, :, 1], sibling)

    def m1(c):
        if c == 0:
            got("x_c0", "x_c1")
            loads[1].wait()
            loads[2].wait()
        for zi in range(2):
            if OFFS[c][zi]:
                got(("xc", c, zi))

        def tile(j, _):
            cols = pl.ds(pl.multiple_of(j * 256, 256), 256)
            r = jnp.dot(x[c].reshape(8 * ROWS, KB), w1[:, cols], preferred_element_type=F32)
            r = r.reshape(4, 2, ROWS, 256)
            p32[c, :, :, :, cols] = r
            p16[c, :, :, :, cols] = r.astype(BF)
            return 0

        lax.fori_loop(0, 7, tile, 0)
        g, u = pl.ds(0, FB), pl.ds(FB, FB)
        send(("u0", c), p16.at[c, :, na, :, u], ux.at[c], across)
        send(("g1r", c), p16.at[c, yo, 0, :, g], gr1.at[c, 0], right)
        send(("g1l", c), p16.at[c, yo, 1, :, g], gr1.at[c, 1], left)
        send(("g2r1", c), p16.at[c, yr, 1, :, g], gr2.at[c, 0, 1], right)
        send(("g2l0", c), p16.at[c, yl, 0, :, g], gr2.at[c, 1, 0], left)

    def s2(c):
        got(("g1r", c))
        sb[c, 0] = (p32[c, yr, 0, :, :FB] + gr1[c, 0].astype(F32)).astype(BF)
        send(("g2r0", c), sb.at[c, 0], gr2.at[c, 0, 0], right)
        got(("g1l", c))
        sb[c, 1] = (p32[c, yl, 1, :, :FB] + gr1[c, 1].astype(F32)).astype(BF)
        send(("g2l1", c), sb.at[c, 1], gr2.at[c, 1, 1], left)
        got(("u0", c))
        for k in range(4):
            q = p32[c, k, a, :, FB:] + ux[c, k].astype(F32)
            q32[c, k] = q
            q16[c, k] = q.astype(BF)
        lo, hi = pl.ds(0, HALF), pl.ds(HALF, FB - HALF)
        send(("u1r", c), q16.at[c, yo, :, lo], ur1.at[c, :, lo], right)
        send(("u1l", c), q16.at[c, yo, :, hi], ur1.at[c, :, hi], left)
        send(("u2rh", c), q16.at[c, yr, :, hi], ur2.at[c, 0, :, hi], right)
        send(("u2ll", c), q16.at[c, yl, :, lo], ur2.at[c, 1, :, lo], left)

    def s3(c):
        got(("g2r0", c), ("g2r1", c), ("g2l0", c), ("g2l1", c))
        t = p32[c, y, na, :, :FB] + gr2[c, 0, na].astype(F32) + gr2[c, 1, na].astype(F32)
        gs[c] = t.astype(BF)
        send(("gx", c), gs.at[c], gx.at[c], across)
        lo, hi = pl.ds(0, HALF), pl.ds(HALF, FB - HALF)
        got(("u1r", c))
        uv[c, :, :HALF] = (q32[c, yr, :, :HALF] + ur1[c, :, :HALF].astype(F32)).astype(BF)
        send(("u2rl", c), uv.at[c, :, lo], ur2.at[c, 0, :, lo], right)
        got(("u1l", c))
        uv[c, :, HALF:] = (q32[c, yl, :, HALF:] + ur1[c, :, HALF:].astype(F32)).astype(BF)
        send(("u2lh", c), uv.at[c, :, hi], ur2.at[c, 1, :, hi], left)

    def s4(c):
        got(("gx", c), ("u2rl", c), ("u2rh", c), ("u2ll", c), ("u2lh", c))
        gate = p32[c, y, a, :, :FB] + gr2[c, 0, a].astype(F32) + gr2[c, 1, a].astype(F32) + gx[c].astype(F32)
        up = q32[c, y] + ur2[c, 0].astype(F32) + ur2[c, 1].astype(F32)
        h[c, y, a] = (gate * jax.nn.sigmoid(gate) * up).astype(BF)
        send(("hx", c), h.at[c, y, a], h.at[c, y, a], across)
        send(("hr", c), h.at[c, y, a], h.at[c, y, a], right)
        send(("hl", c), h.at[c, y, a], h.at[c, y, a], left)

    def a2(c):
        got(("hx", c))
        send(("pr", c), h.at[c, y, na], h.at[c, y, na], right)
        send(("pl", c), h.at[c, y, na], h.at[c, y, na], left)

    def a3(c):
        got(("hr", c))
        send(("fr", c), h.at[c, yl, a], h.at[c, yl, a], right)
        got(("pl", c))
        send(("fl", c), h.at[c, yr, na], h.at[c, yr, na], left)

    def m2(c):
        if c == 0:
            loads[3].wait()
        got(("hl", c), ("pr", c), ("fr", c), ("fl", c))

        def tile(j, _):
            cols = pl.ds(pl.multiple_of(j * 256, 256), 256)
            r = jnp.dot(h[c].reshape(8 * ROWS, FB), w2[:, cols], preferred_element_type=F32)
            o32[c, :, :, :, cols] = r.reshape(4, 2, ROWS, 256)
            return 0

        lax.fori_loop(0, 4, tile, 0)
        send(("c", c), o32.at[c, :, 1], cr.at[c], sibling)

    def g1(c):
        got(("c", c))
        for zi in range(2):
            for dx in range(2):
                k = zi * 2 + dx
                v = o32[c, k, 0] + cr[c, k]
                if OFFS[c][zi] == 0 and dx == 0:
                    own[...] = v
                else:
                    zs[c, k] = v.astype(BF)
                    send(("z", c, k), zs.at[c, k], zr.at[c, k], dev(dz=OFFS[c][zi], dx=dx))

    stages = dict(xf=xf, m1=m1, s2=s2, s3=s3, s4=s4, a2=a2, a3=a3, m2=m2, g1=g1)
    order = sorted((CHUNK_AT[c] + at, c, s) for c in range(CHUNKS) for s, at in STAGE_AT.items())
    for _, c, s in order:
        with jax.named_scope(f"{s}_{c}"):
            stages[s](c)

    total = own[...]
    for c in range(CHUNKS):
        for k in range(4):
            if ("z", c, k) in copies:
                got(("z", c, k))
                total += zr[c, k].astype(F32)
    out[...] = total.astype(BF)
    for cp in copies.values():
        cp.wait_send()


def solution(mesh):
    def step(tokens, gate_weight, up_weight, down_weight):
        c = CHUNKS
        shapes = [
            ((KB, 2 * FB), BF),
            ((FB, KB), BF),
            ((c, 2, 2, 2, ROWS, KB), BF),
            ((c, 4, 2, ROWS, 2 * FB), BF),
            ((c, 4, 2, ROWS, 2 * FB), F32),
            ((c, 2, ROWS, FB), BF),
            ((c, 2, ROWS, FB), BF),
            ((c, 2, 2, ROWS, FB), BF),
            ((c, ROWS, FB), BF),
            ((c, ROWS, FB), BF),
            ((c, 4, ROWS, FB), BF),
            ((c, 4, ROWS, FB), BF),
            ((c, 4, ROWS, FB), F32),
            ((c, ROWS, FB), BF),
            ((c, ROWS, FB), BF),
            ((c, 2, ROWS, FB), BF),
            ((c, 4, 2, ROWS, FB), BF),
            ((c, 4, 2, ROWS, KB), F32),
            ((c, 4, ROWS, KB), F32),
            ((c, 4, ROWS, KB), BF),
            ((c, 4, ROWS, KB), BF),
            ((ROWS, KB), F32),
        ]
        return pl.pallas_call(
            kernel,
            name="swiglu",
            out_shape=jax.ShapeDtypeStruct((ROWS, KB), BF),
            in_specs=[pl.BlockSpec(memory_space=pl.ANY)] * 4,
            out_specs=pl.BlockSpec(memory_space=pltpu.VMEM),
            scratch_shapes=[pltpu.VMEM(s, d) for s, d in shapes]
            + [pltpu.SemaphoreType.DMA((N_SEM,)), pltpu.SemaphoreType.DMA((N_SEM,)), pltpu.SemaphoreType.DMA((4,))],
            compiler_params=pltpu.CompilerParams(collective_id=0, has_side_effects=True, vmem_limit_bytes=60 * 2**20),
        )(tokens, gate_weight, up_weight, down_weight)

    return jax.shard_map(
        step,
        mesh=mesh,
        in_specs=(
            P(("inp", "out"), "wt"),
            P("wt", ("inp", "out")),
            P("wt", ("inp", "out")),
            P(("inp", "out"), "wt"),
        ),
        out_specs=P(("inp", "out"), "wt"),
        check_vma=False,
    )
```

time: 438 us -> 149 us (0.34)
  waiting for transfers between devices: 394 us -> 0 us
  Pallas kernels: 0 us -> 147 us
  matrix products: 23.8 us -> 0 us
  between operations: 13.1 us -> 0.01 us
    reduce_scatter x3 -> x0, waiting for transfers between devices: 261 us -> none  [the longest x1 136 us: shards(): lax.psum_scatter(jnp.dot(hidden_full, down_weight, preferred_element_type...]
    pallas_call x0 -> x1, Pallas kernels: none -> 147 us  [step(): pl.pallas_call(kernel, name='swiglu', out_shape=jax.ShapeDtypeStruct((ROW...]
    all_gather x2 -> x0, waiting for transfers between devices: 132 us -> none  [the longest x1 90.3 us: shards(): all_tokens = lax.all_gather(tokens, ('inp', 'out'), axis=0, tiled=True)]
    dot_general x3 -> x0, matrix products: 23.8 us -> none  [the longest x1 8.35 us: shards(): jnp.dot(all_tokens, gate_weight, preferred_element_type=jnp.float32)]
  transfers between devices with their start and end apart: 5 -> 0, of which waited for: 5 -> 0; matrix products, arithmetic and copies ran while one was open for 2% -> 0% of each run, Pallas kernels for 0% -> 0%
where the time goes in v1:
time: 149 us; the launch traced here: 148 us
  Pallas kernels  147 us (99%)
  local copies, waits for them, and re-layouts  1.54 us (1%)
    pallas_call x1, Pallas kernels, step(): pl.pallas_call(kernel, name='swiglu', out_shape=jax.ShapeDtypeStruct((ROW...  147 us

profile of v1, /device:TPU:1, one launch (start us, length us, event | category | flops | bytes accessed | tf_op | source)
XLA Modules:
  0.0 148.3 jit_solution(12138387014587897378)
XLA Ops:
  0.0 146.8 %swiglu.1 = bf16[48,1024]{1,0:T(8,128)(2,1)} custom-call(bf16[48,1024]{1,0:T(8,128)(2,1)} %tok.1, bf16[1024,896]{1,0:T(8,128)(2,1)} %wg.1, bf16[1024,896]{1,0:T(8,128)(2,1)} %wu.1, bf16[896,1024]{1,0:T(8,128)(2,1)} %wd.1), custom_call_target="tpu_custom_call" | custom-call | tf_op jit(solution)/shard_map/swiglu/pallas_call | solution.py:234
  146.8 1.5 %copy.6 = bf16[48,1024]{1,0:T(8,128)(2,1)} copy(bf16[48,1024]{1,0:T(8,128)(2,1)} %swiglu.1) | data formatting | bytes 196608

commit v2 on v1

--- a/solution.py
+++ b/solution.py
@@ -13,9 +13,13 @@
 FB = 896
 HALF = 512
 CHUNKS = 4
-OFFS = ((0, 1), (-2, 3), (4, -3), (-1, 2))
-STAGE_AT = dict(xf=-1.0, m1=0.0, s2=9.0, s3=14.0, s4=18.0, a2=21.0, a3=24.0, m2=27.0, g1=30.0)
-CHUNK_AT = (0.0, 5.0, 18.0, 31.0)
+OFFS = ((0, -1), (2, -2), (3, 4), (1, -3))
+SLOT = {o: (c, zi) for c, pair in enumerate(OFFS) for zi, o in enumerate(pair)}
+STAGES = ("xr", "m1", "s2", "s3", "s4", "a2", "a3", "m2", "g1")
+ORDER = (
+    2, 3, 4, 10, 5, 6, 11, 7, 20, 9, 13, 12, 21, 23, 31, 33, 22, 41, 32, 51, 43, 61, 30, 53,
+    42, 71, 63, 52, 40, 81, 73, 62, 83, 72, 50, 82, 60, 70, 80,
+)
 N_SEM = 192
 
 
@@ -36,7 +40,7 @@
     right, left, across = (z, a * 4 + yr, ot), (z, a * 4 + yl, ot), (z, na * 4 + y, ot)
 
     loads = [
-        pltpu.make_async_copy(tok, x.at[0, 0, 0, 0], lsem.at[0]),
+        pltpu.make_async_copy(tok, x.at[SLOT[0] + (0, 0)], lsem.at[0]),
         pltpu.make_async_copy(wg, w1.at[:, pl.ds(0, FB)], lsem.at[1]),
         pltpu.make_async_copy(wu, w1.at[:, pl.ds(FB, FB)], lsem.at[2]),
         pltpu.make_async_copy(wd, w2, lsem.at[3]),
@@ -45,11 +49,7 @@
         load.start()
 
     barrier = pltpu.get_barrier_semaphore()
-    peers = [sibling, right, left, across]
-    for dz in range(8):
-        for dx in range(2):
-            if dz or dx:
-                peers.append(dev(dz=dz, dx=dx))
+    peers = [sibling, right, left, across, dev(dx=1), dev(dz=1), dev(dz=-1)]
     for peer in peers:
         pl.semaphore_signal(barrier, inc=1, device_id=peer, device_id_type=MESH)
     pl.semaphore_wait(barrier, len(peers))
@@ -68,31 +68,59 @@
         for name in names:
             copies[name].wait_recv()
 
+    def xs(o, rx, rc):
+        return x.at[SLOT[o] + (rx, rc)]
+
+    def hop(k, rx, step):
+        o = k - step
+        o = 4 if o == -4 else o
+        send(("x", o, rx), xs(k, rx, 0), xs(o, rx, 0), dev(dz=step))
+
     loads[0].wait()
-    send("x_hi", x.at[0, 0, 0, 0], x.at[0, 0, 1, 0], dev(dx=1))
-    send("x_c0", x.at[0, 0, 0, 0], x.at[0, 0, 0, 1], sibling)
+    hop(0, 0, 1)
+    hop(0, 0, -1)
+    send("x_hi", xs(0, 0, 0), xs(0, 1, 0), dev(dx=1))
+    send("x_c0", xs(0, 0, 0), xs(0, 0, 1), sibling)
     got("x_hi")
-    for c in range(CHUNKS):
-        for zi in range(2):
-            o = OFFS[c][zi]
+    hop(0, 1, 1)
+    hop(0, 1, -1)
+    send("x_c1", xs(0, 1, 0), xs(0, 1, 1), sibling)
+
+    def to_sibling(o):
+        c, zi = SLOT[o]
+        send(("xc", o), x.at[c, zi, :, 0], x.at[c, zi, :, 1], sibling)
+
+    def xr(k):
+        k, rx = k // 2, k % 2
+        if k == 4:
+            got(("x", 4, 0), ("x", 4, 1))
+            to_sibling(4)
+            return
+        got(("x", -k, rx))
+        if k < 3 or rx == 0:
+            hop(-k, rx, 1)
+        got(("x", k, rx))
+        if k < 3 or rx == 1:
+            hop(k, rx, -1)
+        if rx == 1:
+            to_sibling(k)
+            to_sibling(-k)
+
+    waited = set()
+
+    def once(*which):
+        for i in which:
+            if i not in waited:
+                waited.add(i)
+                loads[i].wait()
+
+    def m1(c):
+        once(1, 2)
+        for o in OFFS[c]:
             if o:
-                send(("x", c, zi), x.at[0, 0, :, 0], x.at[c, zi, :, 0], dev(dz=-o))
-    send("x_c1", x.at[0, 0, 1, 0], x.at[0, 0, 1, 1], sibling)
-
-    def xf(c):
-        for zi in range(2):
-            if OFFS[c][zi]:
-                got(("x", c, zi))
-                send(("xc", c, zi), x.at[c, zi, :, 0], x.at[c, zi, :, 1], sibling)
-
-    def m1(c):
-        if c == 0:
-            got("x_c0", "x_c1")
-            loads[1].wait()
-            loads[2].wait()
-        for zi in range(2):
-            if OFFS[c][zi]:
-                got(("xc", c, zi))
+                got(("xc", o))
+            else:
+                got("x_c0", "x_c1")
 
         def tile(j, _):
             cols = pl.ds(pl.multiple_of(j * 256, 256), 256)
@@ -162,8 +190,7 @@
         send(("fl", c), h.at[c, yr, na], h.at[c, yr, na], left)
 
     def m2(c):
-        if c == 0:
-            loads[3].wait()
+        once(3)
         got(("hl", c), ("pr", c), ("fr", c), ("fl", c))
 
         def tile(j, _):
@@ -187,9 +214,9 @@
                     zs[c, k] = v.astype(BF)
                     send(("z", c, k), zs.at[c, k], zr.at[c, k], dev(dz=OFFS[c][zi], dx=dx))
 
-    stages = dict(xf=xf, m1=m1, s2=s2, s3=s3, s4=s4, a2=a2, a3=a3, m2=m2, g1=g1)
-    order = sorted((CHUNK_AT[c] + at, c, s) for c in range(CHUNKS) for s, at in STAGE_AT.items())
-    for _, c, s in order:
+    stages = dict(xr=xr, m1=m1, s2=s2, s3=s3, s4=s4, a2=a2, a3=a3, m2=m2, g1=g1)
+    for i in ORDER:
+        s, c = STAGES[i // 10], i % 10
         with jax.named_scope(f"{s}_{c}"):
             stages[s](c)
 

time: 149 us -> 117 us (0.79)
  Pallas kernels: 147 us -> 115 us
    pallas_call x1, Pallas kernels: 147 us -> 115 us  [step(): pl.pallas_call(kernel, name='swiglu', out_shape=jax.ShapeDtypeStruct((ROW...]
where the time goes in v2:
time: 117 us
  Pallas kernels  115 us (98%)
  local copies, waits for them, and re-layouts  1.54 us (1%)
    pallas_call x1, Pallas kernels, step(): pl.pallas_call(kernel, name='swiglu', out_shape=jax.ShapeDtypeStruct((ROW...  115 us

profile of v2, /device:TPU:1, one launch (start us, length us, event | category | flops | bytes accessed | tf_op | source)
XLA Modules:
  0.0 117.0 jit_solution(14901091032004690956)
XLA Ops:
  0.0 115.4 %swiglu.1 = bf16[48,1024]{1,0:T(8,128)(2,1)} custom-call(bf16[48,1024]{1,0:T(8,128)(2,1)} %tok.1, bf16[1024,896]{1,0:T(8,128)(2,1)} %wg.1, bf16[1024,896]{1,0:T(8,128)(2,1)} %wu.1, bf16[896,1024]{1,0:T(8,128)(2,1)} %wd.1), custom_call_target="tpu_custom_call" | custom-call | tf_op jit(solution)/shard_map/swiglu/pallas_call | solution.py:261
  115.5 1.5 %copy.6 = bf16[48,1024]{1,0:T(8,128)(2,1)} copy(bf16[48,1024]{1,0:T(8,128)(2,1)} %swiglu.1) | data formatting | bytes 196608

commit v3 on v2

v3 whole, which is shorter than its diff:
```python
import jax
import jax.numpy as jnp
from jax import lax
from jax.experimental import pallas as pl
from jax.experimental.pallas import tpu as pltpu
from jax.sharding import PartitionSpec as P

MESH = pl.DeviceIdType.MESH
BF, F32 = jnp.bfloat16, jnp.float32

ROWS = 48
KB = 1024
FB = 896
HID = ((0, 512), (512, 384))
COL = ((0, 1024), (1024, 768))
YF = ((0, 640), (640, 384))
XF = ((0, 384), (384, 384))
YW, XW = 1024, 768
LO = 256
CHUNKS = 4
OFFS = ((0, -1), (2, -2), (3, 4), (1, -3))
SLOT = {o: (c, zi) for c, pair in enumerate(OFFS) for zi, o in enumerate(pair)}
STAGES = ("xr", "m1", "s2", "s3", "s4", "a2", "a3", "m2", "g1")
ORDER = (
    2, 3, 4, 10, 5, 11, 6, 12, 7, 13, 20, 21, 9, 22, 15, 14, 23, 32, 25, 16, 33, 42, 24, 17,
    52, 43, 34, 35, 31, 53, 30, 62, 44, 63, 45, 26, 54, 55, 27, 71, 40, 64, 65, 41, 36, 37, 81, 51,
    50, 72, 47, 46, 60, 61, 82, 57, 56, 70, 67, 66, 80, 73, 83,
)
N_SEM = 240


def kernel(tok, wg, wu, wd, out, w1, w2, x, p16, p32, gr1, sb, gr2, gs, gx, ux, q16, q32, ur1, uv, ur2, h, o32, cr, zs, zr, own,
           ssem, rsem, lsem):
    z = lax.axis_index("inp")
    wt = lax.axis_index("wt")
    ot = lax.axis_index("out")
    a, y = wt // 4, wt % 4
    xh, core = ot // 2, ot % 2
    na = 1 - a
    yr, yl, yo = (y + 1) % 4, (y + 3) % 4, (y + 2) % 4

    def dev(dz=0, dx=0, dc=0):
        return (lax.rem(z + dz + 8, 8), wt, (xh + dx) % 2 * 2 + (core + dc) % 2)

    sibling = dev(dc=1)
    right, left, across = (z, a * 4 + yr, ot), (z, a * 4 + yl, ot), (z, na * 4 + y, ot)

    loads = [
        pltpu.make_async_copy(tok, x.at[SLOT[0] + (0, 0)], lsem.at[0]),
        pltpu.make_async_copy(wd, w2, lsem.at[1]),
    ]
    for p in range(2):
        (at, n), col = HID[p], COL[p][0]
        loads.append(pltpu.make_async_copy(wg.at[:, pl.ds(at, n)], w1.at[:, pl.ds(col, n)], lsem.at[2 + 2 * p]))
        loads.append(pltpu.make_async_copy(wu.at[:, pl.ds(at, n)], w1.at[:, pl.ds(col + n, n)], lsem.at[3 + 2 * p]))
    for load in loads:
        load.start()

    barrier = pltpu.get_barrier_semaphore()
    peers = [sibling, right, left, across, dev(dx=1), dev(dz=1), dev(dz=-1)]
    for peer in peers:
        pl.semaphore_signal(barrier, inc=1, device_id=peer, device_id_type=MESH)
    pl.semaphore_wait(barrier, len(peers))

    copies = {}

    def send(name, src, dst, to):
        i = len(copies)
        cp = pltpu.make_async_remote_copy(
            src_ref=src, dst_ref=dst, send_sem=ssem.at[i], recv_sem=rsem.at[i], device_id=to, device_id_type=MESH
        )
        cp.start()
        copies[name] = cp

    def got(*names):
        for name in names:
            copies[name].wait_recv()

    def xs(o, rx, rc):
        return x.at[SLOT[o] + (rx, rc)]

    def hop(k, rx, step):
        o = k - step
        o = 4 if o == -4 else o
        send(("x", o, rx), xs(k, rx, 0), xs(o, rx, 0), dev(dz=step))

    loads[0].wait()
    hop(0, 0, 1)
    hop(0, 0, -1)
    send("x_hi", xs(0, 0, 0), xs(0, 1, 0), dev(dx=1))
    send("x_c0", xs(0, 0, 0), xs(0, 0, 1), sibling)
    got("x_hi")
    hop(0, 1, 1)
    hop(0, 1, -1)
    send("x_c1", xs(0, 1, 0), xs(0, 1, 1), sibling)

    def to_sibling(o):
        c, zi = SLOT[o]
        send(("xc", o), x.at[c, zi, :, 0], x.at[c, zi, :, 1], sibling)

    def xr(k):
        k, rx = k // 2, k % 2
        if k == 4:
            got(("x", 4, 0), ("x", 4, 1))
            to_sibling(4)
            return
        got(("x", -k, rx))
        if k < 3 or rx == 0:
            hop(-k, rx, 1)
        got(("x", k, rx))
        if k < 3 or rx == 1:
            hop(k, rx, -1)
        if rx == 1:
            to_sibling(k)
            to_sibling(-k)

    waited = set()

    def once(*which):
        for i in which:
            if i not in waited:
                waited.add(i)
                loads[i].wait()

    def yf(i, at=0, n=None):
        return pl.ds(YF[i % 2][0] + at, YF[i % 2][1] - at if n is None else n)

    def xf(i, at=0, n=None):
        return pl.ds(XF[i % 2][0] + at, XF[i % 2][1] - at if n is None else n)

    def pcols(i):
        col, width = COL[i % 2]
        n = YF[i % 2][1]
        return pl.ds(col, n), pl.ds(col + n, width - n)

    def hid(i):
        return pl.ds(*HID[i % 2])

    def m1(i):
        c, p = i // 2, i % 2
        once(2 + 2 * p, 3 + 2 * p)
        for o in OFFS[c]:
            if ("xo", o) not in waited:
                waited.add(("xo", o))
                if o:
                    got(("xc", o))
                else:
                    got("x_c0", "x_c1")

        def tile(j, _):
            cols = pl.ds(pl.multiple_of(COL[p][0] + j * 256, 256), 256)
            r = jnp.dot(x[c].reshape(8 * ROWS, KB), w1[:, cols], preferred_element_type=F32)
            r = r.reshape(4, 2, ROWS, 256)
            p32[c, :, :, :, cols] = r
            p16[c, :, :, :, cols] = r.astype(BF)
            return 0

        lax.fori_loop(0, COL[p][1] // 256, tile, 0)
        g, u = pcols(i)
        send(("u0", i), p16.at[c, :, na, :, u], ux.at[c, :, :, xf(i)], across)
        send(("g1r", i), p16.at[c, yo, 0, :, g], gr1.at[c, 0, :, yf(i)], right)
        send(("g1l", i), p16.at[c, yo, 1, :, g], gr1.at[c, 1, :, yf(i)], left)
        send(("g2r1", i), p16.at[c, yr, 1, :, g], gr2.at[c, 0, 1, :, yf(i)], right)
        send(("g2l0", i), p16.at[c, yl, 0, :, g], gr2.at[c, 1, 0, :, yf(i)], left)

    def s2(i):
        c = i // 2
        g, u = pcols(i)
        f, v = yf(i), xf(i)
        got(("g1r", i))
        sb[c, 0, :, f] = (p32[c, yr, 0, :, g] + gr1[c, 0, :, f].astype(F32)).astype(BF)
        send(("g2r0", i), sb.at[c, 0, :, f], gr2.at[c, 0, 0, :, f], right)
        got(("g1l", i))
        sb[c, 1, :, f] = (p32[c, yl, 1, :, g] + gr1[c, 1, :, f].astype(F32)).astype(BF)
        send(("g2l1", i), sb.at[c, 1, :, f], gr2.at[c, 1, 1, :, f], left)
        got(("u0", i))
        for k in range(4):
            q = p32[c, k, a, :, u] + ux[c, k, :, v].astype(F32)
            q32[c, k, :, v] = q
            q16[c, k, :, v] = q.astype(BF)
        lo, hi = xf(i, 0, LO), xf(i, LO)
        send(("u1r", i), q16.at[c, yo, :, lo], ur1.at[c, :, lo], right)
        send(("u1l", i), q16.at[c, yo, :, hi], ur1.at[c, :, hi], left)
        send(("u2rh", i), q16.at[c, yr, :, hi], ur2.at[c, 0, :, hi], right)
        send(("u2ll", i), q16.at[c, yl, :, lo], ur2.at[c, 1, :, lo], left)

    def s3(i):
        c = i // 2
        g, _ = pcols(i)
        f = yf(i)
        got(("g2r0", i), ("g2r1", i), ("g2l0", i), ("g2l1", i))
        t = p32[c, y, na, :, g] + gr2[c, 0, na, :, f].astype(F32) + gr2[c, 1, na, :, f].astype(F32)
        gs[c, :, f] = t.astype(BF)
        send(("gx", i), gs.at[c, :, f], gx.at[c, :, f], across)
        lo, hi = xf(i, 0, LO), xf(i, LO)
        got(("u1r", i))
        uv[c, :, lo] = (q32[c, yr, :, lo] + ur1[c, :, lo].astype(F32)).astype(BF)
        send(("u2rl", i), uv.at[c, :, lo], ur2.at[c, 0, :, lo], right)
        got(("u1l", i))
        uv[c, :, hi] = (q32[c, yl, :, hi] + ur1[c, :, hi].astype(F32)).astype(BF)
        send(("u2lh", i), uv.at[c, :, hi], ur2.at[c, 1, :, hi], left)

    def s4(i):
        c = i // 2
        g, _ = pcols(i)
        f, v, e = yf(i), xf(i), hid(i)
        n = HID[i % 2][1]
        got(("gx", i), ("u2rl", i), ("u2rh", i), ("u2ll", i), ("u2lh", i))
        t = p32[c, y, a, :, g] + gr2[c, 0, a, :, f].astype(F32) + gr2[c, 1, a, :, f].astype(F32) + gx[c, :, f].astype(F32)
        up = q32[c, y, :, v] + ur2[c, 0, :, v].astype(F32) + ur2[c, 1, :, v].astype(F32)
        gate = t[:, :n]
        if YF[i % 2][1] > n:
            up = jnp.concatenate([t[:, n:], up], axis=1)
        h[c, y, a, :, e] = (gate * jax.nn.sigmoid(gate) * up).astype(BF)
        own_h = h.at[c, y, a, :, e]
        send(("hx", i), own_h, own_h, across)
        send(("hr", i), own_h, own_h, right)
        send(("hl", i), own_h, own_h, left)

    def a2(i):
        got(("hx", i))
        block = h.at[i // 2, y, na, :, hid(i)]
        send(("pr", i), block, block, right)
        send(("pl", i), block, block, left)

    def a3(i):
        got(("hr", i))
        block = h.at[i // 2, yl, a, :, hid(i)]
        send(("fr", i), block, block, right)
        got(("pl", i))
        block = h.at[i // 2, yr, na, :, hid(i)]
        send(("fl", i), block, block, left)

    def m2(c):
        once(1)
        for i in (2 * c, 2 * c + 1):
            got(("hl", i), ("pr", i), ("fr", i), ("fl", i))

        def tile(j, _):
            cols = pl.ds(pl.multiple_of(j * 256, 256), 256)
            r = jnp.dot(h[c].reshape(8 * ROWS, FB), w2[:, cols], preferred_element_type=F32)
            o32[c, :, :, :, cols] = r.reshape(4, 2, ROWS, 256)
            return 0

        lax.fori_loop(0, 4, tile, 0)
        send(("c", c), o32.at[c, :, 1], cr.at[c], sibling)

    def g1(c):
        got(("c", c))
        for zi in range(2):
            for dx in range(2):
                k = zi * 2 + dx
                v = o32[c, k, 0] + cr[c, k]
                if OFFS[c][zi] == 0 and dx == 0:
                    own[...] = v
                else:
                    zs[c, k] = v.astype(BF)
                    send(("z", c, k), zs.at[c, k], zr.at[c, k], dev(dz=OFFS[c][zi], dx=dx))

    stages = dict(xr=xr, m1=m1, s2=s2, s3=s3, s4=s4, a2=a2, a3=a3, m2=m2, g1=g1)
    for i in ORDER:
        s, c = STAGES[i // 10], i % 10
        with jax.named_scope(f"{s}_{c}"):
            stages[s](c)

    total = own[...]
    for c in range(CHUNKS):
        for k in range(4):
            if ("z", c, k) in copies:
                got(("z", c, k))
                total += zr[c, k].astype(F32)
    out[...] = total.astype(BF)
    for cp in copies.values():
        cp.wait_send()


def solution(mesh):
    def step(tokens, gate_weight, up_weight, down_weight):
        c = CHUNKS
        shapes = [
            ((KB, 2 * FB), BF),
            ((FB, KB), BF),
            ((c, 2, 2, 2, ROWS, KB), BF),
            ((c, 4, 2, ROWS, 2 * FB), BF),
            ((c, 4, 2, ROWS, 2 * FB), F32),
            ((c, 2, ROWS, YW), BF),
            ((c, 2, ROWS, YW), BF),
            ((c, 2, 2, ROWS, YW), BF),
            ((c, ROWS, YW), BF),
            ((c, ROWS, YW), BF),
            ((c, 4, ROWS, XW), BF),
            ((c, 4, ROWS, XW), BF),
            ((c, 4, ROWS, XW), F32),
            ((c, ROWS, XW), BF),
            ((c, ROWS, XW), BF),
            ((c, 2, ROWS, XW), BF),
            ((c, 4, 2, ROWS, FB), BF),
            ((c, 4, 2, ROWS, KB), F32),
            ((c, 4, ROWS, KB), F32),
            ((c, 4, ROWS, KB), BF),
            ((c, 4, ROWS, KB), BF),
            ((ROWS, KB), F32),
        ]
        return pl.pallas_call(
            kernel,
            name="swiglu",
            out_shape=jax.ShapeDtypeStruct((ROWS, KB), BF),
            in_specs=[pl.BlockSpec(memory_space=pl.ANY)] * 4,
            out_specs=pl.BlockSpec(memory_space=pltpu.VMEM),
            scratch_shapes=[pltpu.VMEM(s, d) for s, d in shapes]
            + [pltpu.SemaphoreType.DMA((N_SEM,)), pltpu.SemaphoreType.DMA((N_SEM,)), pltpu.SemaphoreType.DMA((6,))],
            compiler_params=pltpu.CompilerParams(collective_id=0, has_side_effects=True, vmem_limit_bytes=60 * 2**20),
        )(tokens, gate_weight, up_weight, down_weight)

    return jax.shard_map(
        step,
        mesh=mesh,
        in_specs=(
            P(("inp", "out"), "wt"),
            P("wt", ("inp", "out")),
            P("wt", ("inp", "out")),
            P(("inp", "out"), "wt"),
        ),
        out_specs=P(("inp", "out"), "wt"),
        check_vma=False,
    )
```

time: 117 us -> 113 us (0.966)
  Pallas kernels: 115 us -> 111 us
    pallas_call x1, Pallas kernels: 115 us -> 111 us  [step(): pl.pallas_call(kernel, name='swiglu', out_shape=jax.ShapeDtypeStruct((ROW...]
where the time goes in v3:
time: 113 us
  Pallas kernels  111 us (98%)
  local copies, waits for them, and re-layouts  1.54 us (1%)
    pallas_call x1, Pallas kernels, step(): pl.pallas_call(kernel, name='swiglu', out_shape=jax.ShapeDtypeStruct((ROW...  111 us

profile of v3, /device:TPU:1, one launch (start us, length us, event | category | flops | bytes accessed | tf_op | source)
XLA Modules:
  0.0 112.9 jit_solution(15759595941177024940)
XLA Ops:
  0.0 111.3 %swiglu.1 = bf16[48,1024]{1,0:T(8,128)(2,1)} custom-call(bf16[48,1024]{1,0:T(8,128)(2,1)} %tok.1, bf16[1024,896]{1,0:T(8,128)(2,1)} %wg.1, bf16[1024,896]{1,0:T(8,128)(2,1)} %wu.1, bf16[896,1024]{1,0:T(8,128)(2,1)} %wd.1), custom_call_target="tpu_custom_call" | custom-call | tf_op jit(solution)/shard_map/swiglu/pallas_call | solution.py:304
  111.3 1.5 %copy.6 = bf16[48,1024]{1,0:T(8,128)(2,1)} copy(bf16[48,1024]{1,0:T(8,128)(2,1)} %swiglu.1) | data formatting | bytes 196608

commit v4 on v3

--- a/solution.py
+++ b/solution.py
@@ -18,18 +18,19 @@
 YW, XW = 1024, 768
 LO = 256
 CHUNKS = 4
-OFFS = ((0, -1), (2, -2), (3, 4), (1, -3))
+WIDE = (1, -1)
+OFFS = ((1, -1), (3, -3), (2, 4), (0, -2))
 SLOT = {o: (c, zi) for c, pair in enumerate(OFFS) for zi, o in enumerate(pair)}
-STAGES = ("xr", "m1", "s2", "s3", "s4", "a2", "a3", "m2", "g1")
+STAGES = ("xr", "m1", "s2", "s3", "s4", "a2", "a3", "m2", "g1", "g2")
 ORDER = (
-    2, 3, 4, 10, 5, 11, 6, 12, 7, 13, 20, 21, 9, 22, 15, 14, 23, 32, 25, 16, 33, 42, 24, 17,
-    52, 43, 34, 35, 31, 53, 30, 62, 44, 63, 45, 26, 54, 55, 27, 71, 40, 64, 65, 41, 36, 37, 81, 51,
-    50, 72, 47, 46, 60, 61, 82, 57, 56, 70, 67, 66, 80, 73, 83,
+    2, 3, 4, 11, 5, 10, 6, 17, 21, 7, 16, 20, 13, 9, 12, 26, 31, 30, 14, 15, 41, 23, 40, 27,
+    22, 25, 37, 33, 51, 32, 24, 36, 43, 50, 42, 35, 53, 52, 34, 60, 61, 47, 63, 46, 62, 45, 44, 70,
+    55, 54, 57, 56, 71, 80, 65, 64, 66, 81, 67, 72, 90, 73, 82, 91, 83, 92, 93,
 )
 N_SEM = 240
 
 
-def kernel(tok, wg, wu, wd, out, w1, w2, x, p16, p32, gr1, sb, gr2, gs, gx, ux, q16, q32, ur1, uv, ur2, h, o32, cr, zs, zr, own,
+def kernel(tok, wg, wu, wd, out, w1, w2, x, p16, p32, gr1, sb, gr2, gs, gx, ux, q16, q32, ur1, uv, ur2, h, o32, cr, zs, zr, own, ws, wr,
            ssem, rsem, lsem):
     z = lax.axis_index("inp")
     wt = lax.axis_index("wt")
@@ -242,33 +243,44 @@
             o32[c, :, :, :, cols] = r.reshape(4, 2, ROWS, 256)
             return 0
 
-        lax.fori_loop(0, 4, tile, 0)
-        send(("c", c), o32.at[c, :, 1], cr.at[c], sibling)
+        for half in range(2):
+            lax.fori_loop(2 * half, 2 * half + 2, tile, 0)
+            cols = pl.ds(512 * half, 512)
+            send(("c", c, half), o32.at[c, :, 1, :, cols], cr.at[c, :, :, cols], sibling)
 
     def g1(c):
-        got(("c", c))
+        got(("c", c, 0), ("c", c, 1))
         for zi in range(2):
-            for dx in range(2):
-                k = zi * 2 + dx
-                v = o32[c, k, 0] + cr[c, k]
-                if OFFS[c][zi] == 0 and dx == 0:
-                    own[...] = v
-                else:
-                    zs[c, k] = v.astype(BF)
-                    send(("z", c, k), zs.at[c, k], zr.at[c, k], dev(dz=OFFS[c][zi], dx=dx))
-
-    stages = dict(xr=xr, m1=m1, s2=s2, s3=s3, s4=s4, a2=a2, a3=a3, m2=m2, g1=g1)
+            k = 2 * zi + 1
+            zs[c, k] = (o32[c, k, 0] + cr[c, k]).astype(BF)
+            send(("gh", c, zi), zs.at[c, k], zr.at[c, k], dev(dx=1))
+
+    def g2(c):
+        for zi in range(2):
+            k, o = 2 * zi, OFFS[c][zi]
+            got(("gh", c, zi))
+            v = o32[c, k, 0] + cr[c, k] + zr[c, k + 1].astype(F32)
+            if o == 0:
+                own[...] = v
+            else:
+                source, target = (zs, zr) if o not in WIDE else (ws, wr)
+                i = (c, k) if o not in WIDE else (WIDE.index(o),)
+                source[i] = v.astype(source.dtype)
+                send(("z", c, k), source.at[i], target.at[i], dev(dz=o))
+
+    stages = dict(xr=xr, m1=m1, s2=s2, s3=s3, s4=s4, a2=a2, a3=a3, m2=m2, g1=g1, g2=g2)
     for i in ORDER:
         s, c = STAGES[i // 10], i % 10
         with jax.named_scope(f"{s}_{c}"):
             stages[s](c)
 
     total = own[...]
-    for c in range(CHUNKS):
+    for c in [i % 10 for i in ORDER if STAGES[i // 10] == "g2"]:
         for k in range(4):
             if ("z", c, k) in copies:
                 got(("z", c, k))
-                total += zr[c, k].astype(F32)
+                o = OFFS[c][k // 2]
+                total += wr[WIDE.index(o)] if o in WIDE else zr[c, k].astype(F32)
     out[...] = total.astype(BF)
     for cp in copies.values():
         cp.wait_send()
@@ -300,6 +312,8 @@
             ((c, 4, ROWS, KB), BF),
             ((c, 4, ROWS, KB), BF),
             ((ROWS, KB), F32),
+            ((len(WIDE), ROWS, KB), F32),
+            ((len(WIDE), ROWS, KB), F32),
         ]
         return pl.pallas_call(
             kernel,

time: 113 us -> 112 us (level)
    pallas_call x1, Pallas kernels: 111 us -> 110 us  [step(): pl.pallas_call(kernel, name='swiglu', out_shape=jax.ShapeDtypeStruct((ROW...]
where the time goes in v4:
time: 112 us
  Pallas kernels  110 us (98%)
  local copies, waits for them, and re-layouts  1.54 us (1%)
    pallas_call x1, Pallas kernels, step(): pl.pallas_call(kernel, name='swiglu', out_shape=jax.ShapeDtypeStruct((ROW...  110 us

profile of v4, /device:TPU:1, one launch (start us, length us, event | category | flops | bytes accessed | tf_op | source)
XLA Modules:
  0.0 111.7 jit_solution(14815380844711547818)
XLA Ops:
  0.0 110.1 %swiglu.1 = bf16[48,1024]{1,0:T(8,128)(2,1)} custom-call(bf16[48,1024]{1,0:T(8,128)(2,1)} %tok.1, bf16[1024,896]{1,0:T(8,128)(2,1)} %wg.1, bf16[1024,896]{1,0:T(8,128)(2,1)} %wu.1, bf16[896,1024]{1,0:T(8,128)(2,1)} %wd.1), custom_call_target="tpu_custom_call" | custom-call | tf_op jit(solution)/shard_map/swiglu/pallas_call | solution.py:318
  110.1 1.5 %copy.6 = bf16[48,1024]{1,0:T(8,128)(2,1)} copy(bf16[48,1024]{1,0:T(8,128)(2,1)} %swiglu.1) | data formatting | bytes 196608

commit v5 on v4

--- a/solution.py
+++ b/solution.py
@@ -18,7 +18,7 @@
 YW, XW = 1024, 768
 LO = 256
 CHUNKS = 4
-WIDE = (1, -1)
+WIDE = (1,)
 OFFS = ((1, -1), (3, -3), (2, 4), (0, -2))
 SLOT = {o: (c, zi) for c, pair in enumerate(OFFS) for zi, o in enumerate(pair)}
 STAGES = ("xr", "m1", "s2", "s3", "s4", "a2", "a3", "m2", "g1", "g2")

time: 112 us -> 110 us (0.982)
    pallas_call x1, Pallas kernels: 110 us -> 109 us  [step(): pl.pallas_call(kernel, name='swiglu', out_shape=jax.ShapeDtypeStruct((ROW...]
where the time goes in v5:
time: 110 us
  Pallas kernels  109 us (99%)
  local copies, waits for them, and re-layouts  1.54 us (1%)
    pallas_call x1, Pallas kernels, step(): pl.pallas_call(kernel, name='swiglu', out_shape=jax.ShapeDtypeStruct((ROW...  109 us

profile of v5, /device:TPU:1, one launch (start us, length us, event | category | flops | bytes accessed | tf_op | source)
XLA Modules:
  0.0 110.2 jit_solution(13224993481179563498)
XLA Ops:
  0.0 108.7 %swiglu.1 = bf16[48,1024]{1,0:T(8,128)(2,1)} custom-call(bf16[48,1024]{1,0:T(8,128)(2,1)} %tok.1, bf16[1024,896]{1,0:T(8,128)(2,1)} %wg.1, bf16[1024,896]{1,0:T(8,128)(2,1)} %wu.1, bf16[896,1024]{1,0:T(8,128)(2,1)} %wd.1), custom_call_target="tpu_custom_call" | custom-call | tf_op jit(solution)/shard_map/swiglu/pallas_call | solution.py:318
  108.7 1.5 %copy.6 = bf16[48,1024]{1,0:T(8,128)(2,1)} copy(bf16[48,1024]{1,0:T(8,128)(2,1)} %swiglu.1) | data formatting | bytes 196608
